TPU v7x, 32 devices: a whole 2x2x4 slice. The times are simulated.
32 devices in a mesh: grp: 2 (over y), section: 4 (over x, core), walk: 4 (over z).
Axes of the slice: x: 2, y: 2, z: 4, core: 2. Of those that a mesh axis runs over, the one named last changes fastest.
Arguments:
- states: bfloat16 [4, 4, 8, 128, 256], P('section', None, ('grp', 'walk')), parts along dimension 2, may hold values from -6 to 6
- pair_feats: bfloat16 [4, 8, 32, 16384], P(None, ('grp', 'walk')), parts along dimension 1, may hold values from -6 to 6
- top_cotangent: bfloat16 [4, 8, 128, 256], P(None, ('grp', 'walk')), parts along dimension 1, may hold values from -6 to 6
- w_key: bfloat16 [4, 256, 256], P('section', 'walk'), may hold values from -0.375 to 0.375
- w_msg: bfloat16 [4, 32, 256], P('section', None, 'walk'), may hold values from -1 to 1
- b_msg: float32 [4, 256], P('section'), may hold values from -3 to 3
- w_self: bfloat16 [4, 256, 256], P('section', 'walk'), may hold values from -0.375 to 0.375
- w_up: bfloat16 [4, 256, 256], P('section', 'walk'), may hold values from -0.375 to 0.375
- w_down: bfloat16 [4, 256, 256], P('section', 'walk'), may hold values from -0.375 to 0.375
- b_self: float32 [4, 256], P('section'), may hold values from -3 to 3
- spins: int32 [128], replicated, may hold values from 0 to 1
Outputs:
- dh_layers: bfloat16 [4, 4, 8, 128, 256], P('section', None, ('grp', 'walk')), parts along dimension 2
- grad_key: float32 [8, 256, 256], P(('grp', 'section'), 'walk'), parts along dimension 0
- grad_msg: float32 [8, 32, 256], P(('grp', 'section'), None, 'walk'), parts along dimension 0
- grad_bias_msg: float32 [8, 256], P(('grp', 'section'), 'walk'), parts along dimension 0
- grad_self: float32 [8, 256, 256], P(('grp', 'section'), 'walk'), parts along dimension 0
- grad_up: float32 [8, 256, 256], P(('grp', 'section'), 'walk'), parts along dimension 0
- grad_down: float32 [8, 256, 256], P(('grp', 'section'), 'walk'), parts along dimension 0
- grad_bias_self: float32 [8, 256], P(('grp', 'section'), 'walk'), parts along dimension 0
There are 2 independent parts, one for each index of `grp`. A program takes and returns all parts, laid end to end along the dimension named above; an argument that names none is the same for every part. Nothing has to cross between parts.
Inputs may be any that keep to these rules, and one draw needn't show every extreme that they name: `spins`: each electron's spin label, 0 for up and 1 for down.
All inputs are finite; a program needn't handle non-finite values.
Results may differ from a plain program's by a relative error of at most 0.018.
Values may be sent and summed in bfloat16 or wider, within the bound.
A program may use at most 64 MiB of HBM per device.

v0:
```python
import math

import jax
import jax.numpy as jnp
from jax import lax
from jax.sharding import PartitionSpec as P


def from_behind(shard, axis, by):
    length = lax.axis_size(axis)
    pairs = [(i, i + by) for i in range(length) if 0 <= i + by < length]
    return lax.ppermute(shard, axis, pairs)


def inner_product(left, right):
    return lax.dot_general(
        left, right, (((0,), (0,)), ((), ())), preferred_element_type=jnp.float32
    )


def walker_back(weights, spin_up, spin_pair, state, pairs, incoming):
    w_key, w_msg, b_msg, w_self, w_up, w_down, b_self = weights
    elec = state.shape[0]
    width = state.shape[1]
    pair_width = pairs.shape[0]
    block = math.gcd(elec, max(1, 2048 // elec))
    blocks = elec // block
    keyed = jnp.dot(state, w_key, preferred_element_type=jnp.float32)

    def row_block(carry, index):
        dkey_sum, grad_message, bias_message, grad_self, grad_up, grad_down, bias_self = carry
        start = index * block
        pair_block = lax.dynamic_slice_in_dim(pairs, start * elec, block * elec, 1)
        state_block = lax.dynamic_slice_in_dim(state, start, block, 0)
        incoming_block = lax.dynamic_slice_in_dim(incoming, start, block, 0)
        pre_msg = inner_product(pair_block, w_msg).reshape(block, elec, width)
        pre_msg = pre_msg + keyed[None, :, :] + b_msg[None, None, :]
        message = jnp.tanh(pre_msg).astype(jnp.bfloat16)
        spin_sums = (
            jnp.einsum("ijd,js->sid", message, spin_pair, preferred_element_type=jnp.float32)
            * (2.0 / elec)
        ).astype(jnp.bfloat16)
        sum_up = spin_sums[0]
        sum_down = spin_sums[1]
        zvalue = jnp.dot(state_block, w_self, preferred_element_type=jnp.float32)
        zvalue = zvalue + jnp.dot(sum_up, w_up, preferred_element_type=jnp.float32)
        zvalue = (
            zvalue + jnp.dot(sum_down, w_down, preferred_element_type=jnp.float32) + b_self[None, :]
        )
        tanh_z = jnp.tanh(zvalue)
        dzeta = (incoming_block.astype(jnp.float32) * (1.0 - tanh_z * tanh_z)).astype(jnp.bfloat16)
        dsum_up = jnp.dot(dzeta, w_up.T, preferred_element_type=jnp.float32)
        dsum_down = jnp.dot(dzeta, w_down.T, preferred_element_type=jnp.float32)
        msg_float = message.astype(jnp.float32)
        spread = (
            dsum_up[:, None, :] * spin_up[None, :, None]
            + dsum_down[:, None, :] * (1.0 - spin_up)[None, :, None]
        )
        dpre = (2.0 / elec * spread * (1.0 - msg_float * msg_float)).astype(jnp.bfloat16)
        dpre_rows = dpre.reshape(block * elec, width)
        carry = (
            dkey_sum + jnp.sum(dpre, axis=0, dtype=jnp.float32),
            grad_message + jnp.dot(pair_block, dpre_rows, preferred_element_type=jnp.float32),
            bias_message + jnp.sum(dpre_rows, axis=0, dtype=jnp.float32),
            grad_self + inner_product(state_block, dzeta),
            grad_up + inner_product(sum_up, dzeta),
            grad_down + inner_product(sum_down, dzeta),
            bias_self + jnp.sum(dzeta, axis=0, dtype=jnp.float32),
        )
        return (carry, dzeta)

    start_carry = (
        jnp.zeros((elec, width), jnp.float32),
        jnp.zeros((pair_width, width), jnp.float32),
        jnp.zeros((width,), jnp.float32),
        jnp.zeros((width, width), jnp.float32),
        jnp.zeros((width, width), jnp.float32),
        jnp.zeros((width, width), jnp.float32),
        jnp.zeros((width,), jnp.float32),
    )
    sums, dzetas = lax.scan(row_block, start_carry, jnp.arange(blocks, dtype=jnp.int32))
    dzeta_all = dzetas.reshape(elec, width)
    dkey = sums[0].astype(jnp.bfloat16)
    dstate = incoming.astype(jnp.float32) + jnp.dot(
        dzeta_all, w_self.T, preferred_element_type=jnp.float32
    )
    dstate = (dstate + jnp.dot(dkey, w_key.T, preferred_element_type=jnp.float32)).astype(
        jnp.bfloat16
    )
    terms = (inner_product(state, dkey), sums[1], sums[2], sums[3], sums[4], sums[5], sums[6])
    return (dstate, terms)


def per_device(
    states, pair_feats, top_cotangent, w_key, w_msg, b_msg, w_self, w_up, w_down, b_self, spins
):
    micro, walkers, elec, width = states.shape[1:]
    pair_width = pair_feats.shape[2]
    local_states = states[0].reshape(micro * walkers, elec, width)
    local_pairs = pair_feats.reshape(micro * walkers, pair_width, elec * elec)
    local_top = top_cotangent.reshape(micro * walkers, elec, width)
    full_key, full_self, full_up, full_down, full_msg = (
        lax.all_gather(w_key, "walk", axis=1, tiled=True),
        lax.all_gather(w_self, "walk", axis=1, tiled=True),
        lax.all_gather(w_up, "walk", axis=1, tiled=True),
        lax.all_gather(w_down, "walk", axis=1, tiled=True),
        lax.all_gather(w_msg, "walk", axis=2, tiled=True),
    )
    weights = (
        full_key[0],
        full_msg[0],
        b_msg[0],
        full_self[0],
        full_up[0],
        full_down[0],
        b_self[0],
    )
    spin_up = (spins == 0).astype(jnp.float32)
    spin_pair = jnp.stack([spin_up, 1.0 - spin_up], axis=1).astype(jnp.bfloat16)
    n_section = lax.axis_size("section")
    section_no = lax.axis_index("section")
    grouped = 1
    per_unit = walkers * grouped
    units = micro // grouped
    ticks = units + n_section - 1

    def run_unit(unit_states, unit_pairs, unit_incoming, grads):

        def step(totals, items):
            state, pairs, incoming = items
            dstate, terms = walker_back(weights, spin_up, spin_pair, state, pairs, incoming)
            return (tuple((total + term for total, term in zip(totals, terms))), dstate)

        return lax.scan(step, grads, (unit_states, unit_pairs, unit_incoming))

    def tick(tick_no, carry):
        received, store, grads = carry
        unit = tick_no - (n_section - 1 - section_no)
        active = jnp.logical_and(unit >= 0, unit < units)
        clipped = jnp.clip(unit, 0, units - 1)
        offset = clipped * per_unit
        from_top = lax.dynamic_slice_in_dim(local_top, offset, per_unit, 0)
        incoming = jnp.where(section_no == n_section - 1, from_top, received)

        def work(operand):
            old_store, old_grads = operand
            unit_states = lax.dynamic_slice_in_dim(local_states, offset, per_unit, 0)
            unit_pairs = lax.dynamic_slice_in_dim(local_pairs, offset, per_unit, 0)
            new_grads, dstates = run_unit(unit_states, unit_pairs, incoming, old_grads)
            new_store = lax.dynamic_update_slice_in_dim(old_store, dstates, offset, 0)
            return (dstates, new_store, new_grads)

        def skip(operand):
            old_store, old_grads = operand
            return (jnp.zeros((per_unit, elec, width), jnp.bfloat16), old_store, old_grads)

        sent, store, grads = lax.cond(active, work, skip, (store, grads))
        received = from_behind(sent, "section", -1)
        return (received, store, grads)

    init_grads = (
        jnp.zeros((width, width), jnp.float32),
        jnp.zeros((pair_width, width), jnp.float32),
        jnp.zeros((width,), jnp.float32),
        jnp.zeros((width, width), jnp.float32),
        jnp.zeros((width, width), jnp.float32),
        jnp.zeros((width, width), jnp.float32),
        jnp.zeros((width,), jnp.float32),
    )
    init = (
        jnp.zeros((per_unit, elec, width), jnp.bfloat16),
        jnp.zeros((micro * walkers, elec, width), jnp.bfloat16),
        init_grads,
    )
    received, store, grads = lax.fori_loop(0, ticks, tick, init)
    summed = (
        lax.psum_scatter(
            grads[0].astype(jnp.bfloat16), "walk", scatter_dimension=0, tiled=True
        ).astype(jnp.float32),
        lax.psum_scatter(
            grads[1].astype(jnp.bfloat16), "walk", scatter_dimension=1, tiled=True
        ).astype(jnp.float32),
        lax.psum_scatter(
            grads[2].astype(jnp.bfloat16), "walk", scatter_dimension=0, tiled=True
        ).astype(jnp.float32),
        lax.psum_scatter(
            grads[3].astype(jnp.bfloat16), "walk", scatter_dimension=0, tiled=True
        ).astype(jnp.float32),
        lax.psum_scatter(
            grads[4].astype(jnp.bfloat16), "walk", scatter_dimension=0, tiled=True
        ).astype(jnp.float32),
        lax.psum_scatter(
            grads[5].astype(jnp.bfloat16), "walk", scatter_dimension=0, tiled=True
        ).astype(jnp.float32),
        lax.psum_scatter(
            grads[6].astype(jnp.bfloat16), "walk", scatter_dimension=0, tiled=True
        ).astype(jnp.float32),
    )
    scaled = [(part / elec)[None] for part in summed]
    dh_local = store.reshape(1, micro, walkers, elec, width)
    return (dh_local, scaled[0], scaled[1], scaled[2], scaled[3], scaled[4], scaled[5], scaled[6])


def solution(mesh):
    in_specs = (
        P("section", None, ("grp", "walk"), None, None),
        P(None, ("grp", "walk"), None, None),
        P(None, ("grp", "walk"), None, None),
        P("section", "walk", None),
        P("section", None, "walk"),
        P("section", None),
        P("section", "walk", None),
        P("section", "walk", None),
        P("section", "walk", None),
        P("section", None),
        P(),
    )
    out_specs = (
        P("section", None, ("grp", "walk"), None, None),
        P(("grp", "section"), "walk", None),
        P(("grp", "section"), None, "walk"),
        P(("grp", "section"), "walk"),
        P(("grp", "section"), "walk", None),
        P(("grp", "section"), "walk", None),
        P(("grp", "section"), "walk", None),
        P(("grp", "section"), "walk"),
    )
    return jax.shard_map(
        per_device, mesh=mesh, in_specs=in_specs, out_specs=out_specs, check_vma=False
    )
```

profile of v0, /device:TPU:0, one launch (start us, length us, event | category | flops | bytes accessed | tf_op | source)
XLA Modules:
  0.0 1385.3 jit_solution(10363217559433560013)
XLA Ops:
  9.9 15.1 %all_gather.17 = bf16[1,32,256]{1,0,2:T(2,128)(2,1)S(1)} all-gather(bf16[1,32,64]{1,0,2:T(2,128)(2,1)S(1)} %copy.21), channel_id=1, replica_groups=mesh['grp'=2,'section'=4,'walk'=4] {'walk'}, dimensions={2}, use_global_device_ids=true | all-gather | bytes 20480 | tf_op jit(solution)/shard_map/all_gather | solution.py:107
  25.7 13.8 all_gather.18
  39.4 13.5 all_gather.19
  53.0 15.9 %all_gather.15 = bf16[1,256,256]{2,1,0:T(8,128)(2,1)} all-gather(bf16[1,64,256]{2,1,0:T(8,128)(2,1)} %param.20), channel_id=1, replica_groups=mesh['grp'=2,'section'=4,'walk'=4] {'walk'}, dimensions={1}, use_global_device_ids=true | all-gather | bytes 163840 | tf_op jit(solution)/shard_map/all_gather | solution.py:103
  68.9 13.5 all_gather.16
  88.3 1191.7 %while.106 = (s32[]{:T(128)}, bf16[1,128,256]{2,1,0:T(8,128)(2,1)S(1)}, bf16[4,128,256]{2,1,0:T(8,128)(2,1)}, f32[256,256]{1,0:T(8,128)}, f32[32,256]{1,0:T(8,12...) while((s32[]{:T(128)}, ...), condition=%wide.region_8.9_spmd, body=%wide.region_0.8_spmd.sunk | while | flops 170345600 | bytes 21800484 | solution.py:175
  94.2 3.9 collective-permute-done
  100.0 488.6 %collective-permute-done = bf16[1,128,256]{2,1,0:T(8,128)(2,1)S(1)} collective-permute-done((bf16[1,128,256]{2,1,0:T(8,128)(2,1)}, bf16[1,128,256]{2,1,0:T(8,128)(2,1)S(1)}, u32[]{:S(2)}, u32[]{:S(2)}) %collective-permute-start) | collective-permute-done | bytes 65568 | tf_op jit(solution)/shard_map/while/body/eval_jaxpr/ppermute | solution.py:12
  588.6 167.7 %conditional.2 = (bf16[1,128,256]{2,1,0:T(8,128)(2,1)}, bf16[4,128,256]{2,1,0:T(8,128)(2,1)}, f32[256,256]{1,0:T(8,128)}, f32[32,256]{1,0:T(8,128)}, f32[256]{0:...) conditional(s32[]{:T(128)} %convert_element_type.244, ...), branch_computations={%region_1.1_spmd, %region_2.7_spmd} | conditional | flops 170345600 | bytes 21537776 | solution.py:157
  594.1 148.6 %while.105 = (s32[]{:T(128)}, f32[128,256]{1,0:T(8,128)S(1)}, f32[32,256]{1,0:T(8,128)}, f32[256]{0:T(256)}, f32[256,256]{1,0:T(8,128)S(1)}, /*index=5*/f32[256,...) while((s32[]{:T(128)}, f32[128,256]{1,0:T(8,128)S(1)}, ...), condition=%wide.region_7.6_spmd.clone, body=%wide.region_3.5_spmd.clone.sunk | while | flops 102736520 | bytes 14412328 | solution.py:81
  757.6 4.5 collective-permute-done
  762.1 167.7 %conditional.2 = (bf16[1,128,256]{2,1,0:T(8,128)(2,1)}, bf16[4,128,256]{2,1,0:T(8,128)(2,1)}, f32[256,256]{1,0:T(8,128)}, f32[32,256]{1,0:T(8,128)}, f32[256]{0:...) conditional(s32[]{:T(128)} %convert_element_type.244, ...), branch_computations={%region_1.1_spmd, %region_2.7_spmd} | conditional | flops 170345600 | bytes 21537776 | solution.py:157
  767.6 148.6 %while.105 = (s32[]{:T(128)}, f32[128,256]{1,0:T(8,128)S(1)}, f32[32,256]{1,0:T(8,128)}, f32[256]{0:T(256)}, f32[256,256]{1,0:T(8,128)S(1)}, /*index=5*/f32[256,...) while((s32[]{:T(128)}, f32[128,256]{1,0:T(8,128)S(1)}, ...), condition=%wide.region_7.6_spmd.clone, body=%wide.region_3.5_spmd.clone.sunk | while | flops 102736520 | bytes 14412328 | solution.py:81
  931.0 4.5 collective-permute-done
  935.5 167.7 %conditional.2 = (bf16[1,128,256]{2,1,0:T(8,128)(2,1)}, bf16[4,128,256]{2,1,0:T(8,128)(2,1)}, f32[256,256]{1,0:T(8,128)}, f32[32,256]{1,0:T(8,128)}, f32[256]{0:...) conditional(s32[]{:T(128)} %convert_element_type.244, ...), branch_computations={%region_1.1_spmd, %region_2.7_spmd} | conditional | flops 170345600 | bytes 21537776 | solution.py:157
  941.0 148.6 %while.105 = (s32[]{:T(128)}, f32[128,256]{1,0:T(8,128)S(1)}, f32[32,256]{1,0:T(8,128)}, f32[256]{0:T(256)}, f32[256,256]{1,0:T(8,128)S(1)}, /*index=5*/f32[256,...) while((s32[]{:T(128)}, f32[128,256]{1,0:T(8,128)S(1)}, ...), condition=%wide.region_7.6_spmd.clone, body=%wide.region_3.5_spmd.clone.sunk | while | flops 102736520 | bytes 14412328 | solution.py:81
  1104.5 4.5 collective-permute-done
  1109.0 167.7 %conditional.2 = (bf16[1,128,256]{2,1,0:T(8,128)(2,1)}, bf16[4,128,256]{2,1,0:T(8,128)(2,1)}, f32[256,256]{1,0:T(8,128)}, f32[32,256]{1,0:T(8,128)}, f32[256]{0:...) conditional(s32[]{:T(128)} %convert_element_type.244, ...), branch_computations={%region_1.1_spmd, %region_2.7_spmd} | conditional | flops 170345600 | bytes 21537776 | solution.py:157
  1114.5 148.6 %while.105 = (s32[]{:T(128)}, f32[128,256]{1,0:T(8,128)S(1)}, f32[32,256]{1,0:T(8,128)}, f32[256]{0:T(256)}, f32[256,256]{1,0:T(8,128)S(1)}, /*index=5*/f32[256,...) while((s32[]{:T(128)}, f32[128,256]{1,0:T(8,128)S(1)}, ...), condition=%wide.region_7.6_spmd.clone, body=%wide.region_3.5_spmd.clone.sunk | while | flops 102736520 | bytes 14412328 | solution.py:81
  1289.5 9.9 all-reduce.2
  1302.7 16.0 %reduce-scatter.14.cloned.1.call-done = bf16[64,256]{1,0:T(8,128)(2,1)} async-done(((bf16[256,256]{1,0:T(8,128)(2,1)}), bf16[64,256]{1,0:T(8,128)(2,1)}) %reduce-scatter.14.cloned.1.call-update) | async-done | bytes 32784 | tf_op jit(solution)/shard_map/reduce_scatter | solution.py:192
  1320.1 18.2 %reduce-scatter.12.cloned.1.call-done = bf16[64,256]{1,0:T(8,128)(2,1)} async-done(((bf16[256,256]{1,0:T(8,128)(2,1)}), bf16[64,256]{1,0:T(8,128)(2,1)}) %reduce-scatter.12.cloned.1.call-update) | async-done | bytes 32784 | tf_op jit(solution)/shard_map/reduce_scatter | solution.py:189
  1339.7 18.2 %reduce-scatter.10.cloned.1.call-done = bf16[64,256]{1,0:T(8,128)(2,1)} async-done(((bf16[256,256]{1,0:T(8,128)(2,1)}), bf16[64,256]{1,0:T(8,128)(2,1)}) %reduce-scatter.10.cloned.1.call-update) | async-done | bytes 32784 | tf_op jit(solution)/shard_map/reduce_scatter | solution.py:186
  1359.3 18.1 %reduce-scatter.8.cloned.1.call-done = bf16[64,256]{1,0:T(8,128)(2,1)} async-done(((bf16[256,256]{1,0:T(8,128)(2,1)}), bf16[64,256]{1,0:T(8,128)(2,1)}) %reduce-scatter.8.cloned.1.call-update) | async-done | bytes 32784 | tf_op jit(solution)/shard_map/reduce_scatter | solution.py:177
  (1222 shorter events, 665.8 us)
Async XLA Ops:
  7.2 1294.1 %reduce-scatter.16.cloned.1.call-start = ((), (), s32[]{:S(2)}) async-start(), calls=%async_computation.9 | async-start | bytes 81920
  89.0 3.3 collective-permute-start
  92.9 5.2 collective-permute-start
  98.7 489.9 %collective-permute-start = (bf16[1,128,256]{2,1,0:T(8,128)(2,1)}, bf16[1,128,256]{2,1,0:T(8,128)(2,1)S(1)}, u32[]{:S(2)}, u32[]{:S(2)}) collective-permute-start(bf16[1,128,256]{2,1,0:T(8,128)(2,1)} %get-tuple-element.1658), channel_id=1, source_target_pairs={{4,0},{8,4},{12,8},{5,1},{9,5},{13,9},{6,2},{10,6},{14,10},{7,3},{... | collective-permute-start | bytes 196616 | tf_op jit(solution)/shard_map/while/body/eval_jaxpr/ppermute | solution.py:12
  621.4 4.3 copy-start.3
  621.4 4.3 copy-start.6
  640.0 4.3 copy-start.3
  742.7 11.2 copy-start.5
  742.7 12.4 copy-start.8
  756.3 5.8 collective-permute-start
  916.2 11.2 copy-start.5
  916.2 12.4 copy-start.8
  929.7 5.8 collective-permute-start
  1089.6 11.2 copy-start.5
  1089.6 12.4 copy-start.8
  1103.2 5.8 collective-permute-start
  1263.1 11.2 copy-start.5
  1263.1 12.4 copy-start.8
  1276.6 3.3 collective-permute-start
  1280.0 19.5 %copy-start.9 = (u32[32]{0:T(128)S(1)}, u32[32]{0:T(128)}, u32[]{:S(2)}) copy-start(u32[32]{0:T(128)} %constant.186) | copy-start | bytes 388
  1281.5 37.2 %reduce-scatter.14.cloned.1.call-start = ((), (), s32[]{:S(2)}) async-start(), calls=%async_computation.8 | async-start | bytes 163840 | tf_op jit(solution)/shard_map/reduce_scatter | solution.py:192
  1283.2 55.1 %reduce-scatter.12.cloned.1.call-start = ((), (), s32[]{:S(2)}) async-start(), calls=%async_computation.7 | async-start | bytes 163840 | tf_op jit(solution)/shard_map/reduce_scatter | solution.py:189
  1284.9 73.0 %reduce-scatter.10.cloned.1.call-start = ((), (), s32[]{:S(2)}) async-start(), calls=%async_computation.6 | async-start | bytes 163840 | tf_op jit(solution)/shard_map/reduce_scatter | solution.py:186
  1286.6 90.8 %reduce-scatter.8.cloned.1.call-start = ((), (), s32[]{:S(2)}) async-start(), calls=%async_computation.5 | async-start | bytes 163840 | tf_op jit(solution)/shard_map/reduce_scatter | solution.py:177
  (193 other events, 496.3 us)
Sparse Core Ops, SparseCore 0:
  1281.6 17.2 reduce-scatter.15
  1301.3 17.3 reduce-scatter.13
  1320.9 17.3 reduce-scatter.11
  1340.5 17.3 reduce-scatter.9
  1360.0 17.3 reduce-scatter.7
where the time goes:
time: 1400 us; the launch traced here: 1390 us
  waiting for transfers between devices  581 us (42%)
  matrix products  325 us (23%)
  other arithmetic  181 us (13%)
  local copies, waits for them, and re-layouts  144 us (10%)
  blocking collectives  81.8 us (6%)
  loops' own time  48.8 us (3%)
  between operations  14.5 us (1%)
    ppermute x7, waiting for transfers between devices, from_behind(): return lax.ppermute(shard, axis, pairs)  510 us
    dot_general x132, matrix products, inner_product(): lax.dot_general(left, right, (((0,), (0,)), ((), ())), preferred_element_...  146 us
    dot_general x32, matrix products, row_block(): jnp.dot(pair_block, dpre_rows, preferred_element_type=jnp.float32)  57.5 us
    reduce_sum x32, other arithmetic, row_block(): jnp.sum(dpre_rows, axis=0, dtype=jnp.float32)  50.7 us
    another operation x4, loops' own time, walker_back(): lax.scan(row_block, start_carry, jnp.arange(blocks, dtype=jnp.int32))  48.5 us
    reduce_sum x32, other arithmetic, row_block(): jnp.sum(dpre, axis=0, dtype=jnp.float32)  46.9 us
    dynamic_slice x32, local copies, waits for them, and re-layouts, walker_back(): lax.scan(row_block, start_carry, jnp.arange(blocks, dtype=jnp.int32))  42.3 us
    add x24, other arithmetic, step(): return (tuple((total + term for total, term in zip(totals, terms))), dstate)  35.1 us
  transfers between devices with their start and end apart: 12, of which 11 were waited for; matrix products, arithmetic and copies ran while one was open for 1% of the time, Pallas kernels for 0%

commit v1 on v0

v1 whole, which is shorter than its diff:
```python
import functools

import jax
import jax.numpy as jnp
from jax import lax
from jax.experimental import pallas as pl
from jax.experimental.pallas import tpu as pltpu
from jax.sharding import PartitionSpec as P

F32 = jnp.float32
BF16 = jnp.bfloat16
MESH = pl.DeviceIdType.MESH


def dot(left, right):
    return jnp.dot(left, right, preferred_element_type=F32)


def dot_tn(left, right):
    return lax.dot_general(left, right, (((0,), (0,)), ((), ())), preferred_element_type=F32)


def dot_nt(left, right):
    return lax.dot_general(left, right, (((1,), (1,)), ((), ())), preferred_element_type=F32)


def join_rows(pieces):
    if pieces[0].shape[0] % 16:
        return jnp.concatenate([piece.astype(F32) for piece in pieces], axis=0).astype(BF16)
    return jnp.concatenate(pieces, axis=0)


def kernel(
    n_walk, n_section,
    states, pairs_hbm, top, wk, wm, bm, ws, wu, wd, bs, spins,
    dh, gk, gm, gbm, gs, gu, gd, gbs,
    slope, pairs, got_key, got_rest, got_msg, full_w, rhs, onehot, spin_rows, up_rows,
    sum_up_f, sum_down_f, sums, tz, arrived, dzs, dkeys, ds_up, ds_down,
    out_rest, in_rest, out_key, in_key, out_msg, in_msg,
    pair_sem, w_send, w_recv, p_send, p_recv, g_send, g_recv,
):
    walk = lax.axis_index("walk")
    section = lax.axis_index("section")
    micro, elec, width = states.shape
    pair_width = pairs.shape[1]
    rows = wk.shape[0]
    cols = wm.shape[1]
    scale = 2.0 / elec
    chunk = 8 * elec
    tile = 2 * elec
    chunks = elec // 8

    for w in range(micro):
        pltpu.make_async_copy(pairs_hbm.at[w], pairs.at[w], pair_sem.at[w]).start()

    peers = [lax.rem(walk + step, n_walk) for step in range(1, n_walk)]
    barrier = pltpu.get_barrier_semaphore()
    for peer in peers:
        pl.semaphore_signal(barrier, inc=1, device_id={"walk": peer}, device_id_type=MESH)
    above = lax.rem(section + 1, n_section)
    below = lax.rem(section + n_section - 1, n_section)
    pl.semaphore_signal(barrier, inc=1, device_id={"section": above}, device_id_type=MESH)
    pl.semaphore_signal(barrier, inc=1, device_id={"section": below}, device_id_type=MESH)

    got_key[walk] = wk[...]
    got_rest[walk, 0] = ws[...]
    got_rest[walk, 1] = wu[...]
    got_rest[walk, 2] = wd[...]
    got_msg[walk] = jnp.concatenate([wm[...], jnp.zeros((pair_width, 128 - cols), BF16)], axis=1)

    pl.semaphore_wait(barrier, n_walk + 1)

    def weight_copy(kind, ref, step, slot):
        return pltpu.make_async_remote_copy(
            src_ref=ref.at[slot], dst_ref=ref.at[slot],
            send_sem=w_send.at[kind, step], recv_sem=w_recv.at[kind, slot],
            device_id={"walk": peers[step]}, device_id_type=MESH,
        )

    kinds = ((0, got_key), (1, got_msg), (2, got_rest))
    for kind, ref in kinds:
        for step in range(n_walk - 1):
            weight_copy(kind, ref, step, walk).start()

    q = lax.broadcasted_iota(jnp.int32, (tile, elec), 0)
    j = lax.broadcasted_iota(jnp.int32, (tile, elec), 1)
    onehot[...] = jnp.where(lax.rem(q, elec) == j, 1.0, 0.0).astype(BF16)
    up = jnp.where(spins[...] == 0, 1.0, 0.0)
    up_both = jnp.concatenate([up, up], axis=1)
    r = lax.broadcasted_iota(jnp.int32, (16, tile), 0)
    q = lax.broadcasted_iota(jnp.int32, (16, tile), 1)
    chosen = jnp.where(r < 8, up_both, 1.0 - up_both)
    for k in range(4):
        spin_rows[k] = jnp.where(q // elec == lax.rem(r, 8) - 2 * k, chosen, 0.0).astype(BF16)
    up_column = jnp.transpose(jnp.broadcast_to(up, (elec, elec)))
    up_rows[...] = jnp.concatenate([up_column] * (width // elec), axis=1).astype(BF16)

    @pl.when(section == n_section - 1)
    def _():
        arrived[...] = top[...]

    for kind, ref in kinds[:2]:
        for step in range(n_walk - 1):
            weight_copy(kind, ref, step, peers[step]).wait_recv()
    full_w[0] = join_rows([got_key[k] for k in range(n_walk)])
    w_msg = jnp.concatenate([got_msg[k][:, :cols] for k in range(n_walk)], axis=1)
    for k in range(4):
        before = [jnp.zeros((k * pair_width, width), BF16)] if k else []
        after = [jnp.zeros(((3 - k) * pair_width, width), BF16)] if k < 3 else []
        rhs[k, 0:elec] = jnp.concatenate(before + [w_msg] + after, axis=0)

    def messages(w, _):
        pltpu.make_async_copy(pairs_hbm.at[w], pairs.at[w], pair_sem.at[w]).wait()
        keyed = (dot(states[w], full_w[0]) + bm[...]).astype(BF16)
        for k in range(4):
            rhs[k, elec:] = keyed

        def step(c, _):
            start = pl.multiple_of(c * chunk, chunk)
            block = pairs[w, :, pl.ds(start, chunk)]
            stacked = jnp.concatenate([block[:, k * tile:(k + 1) * tile] for k in range(4)], axis=0)
            left = jnp.concatenate([jnp.transpose(stacked), onehot[...]], axis=1)
            total = jnp.zeros((16, width), F32)
            for k in range(4):
                message = jnp.tanh(dot(left, rhs[k]).astype(BF16))
                slope[w, pl.ds(start + k * tile, tile), :] = 1.0 - message * message
                total = total + dot(spin_rows[k], message)
            at = pl.ds(pl.multiple_of(c * 8, 8), 8)
            sum_up_f[w, at, :] = total[:8] * scale
            sum_down_f[w, at, :] = total[8:] * scale
            return 0

        lax.fori_loop(0, chunks, step, 0)
        return 0

    lax.fori_loop(0, micro, messages, 0)

    for step in range(n_walk - 1):
        weight_copy(2, got_rest, step, peers[step]).wait_recv()
    for which in range(3):
        full_w[1 + which] = join_rows([got_rest[k, which] for k in range(n_walk)])
    flat = (micro * elec, width)
    sums[0] = sum_up_f[...].reshape(flat).astype(BF16)
    sums[1] = sum_down_f[...].reshape(flat).astype(BF16)
    h_all = states[...].reshape(flat)
    z = dot(h_all, full_w[1]) + dot(sums[0], full_w[2]) + dot(sums[1], full_w[3]) + bs[...]
    tanh_z = jnp.tanh(z)
    tz[...] = (1.0 - tanh_z * tanh_z).reshape(micro, elec, width)

    def down(w):
        return pltpu.make_async_remote_copy(
            src_ref=dh.at[w], dst_ref=arrived.at[w],
            send_sem=p_send.at[w], recv_sem=p_recv.at[w],
            device_id={"section": below}, device_id_type=MESH,
        )

    def grad_copy(kind, out, into, step, target, slot):
        return pltpu.make_async_remote_copy(
            src_ref=out.at[target], dst_ref=into.at[slot],
            send_sem=g_send.at[kind, step], recv_sem=g_recv.at[kind, slot],
            device_id={"walk": peers[step]}, device_id_type=MESH,
        )

    def walker(w, carry):
        grad_msg, bias_msg, bias_self = carry

        @pl.when(section < n_section - 1)
        def _():
            down(w).wait_recv()

        incoming = arrived[w].astype(F32)
        dz = (incoming * tz[w]).astype(BF16)
        here = pl.ds(pl.multiple_of(w * elec, elec), elec)
        dzs[here, :] = dz
        ds_up[...] = dot_nt(dz, full_w[2]) * scale
        ds_down[...] = dot_nt(dz, full_w[3]) * scale

        def step(c, carry):
            dkey, grad = carry
            at = pl.ds(pl.multiple_of(c * 8, 8), 8)
            row_up = ds_up[at, :]
            row_down = ds_down[at, :]
            start = pl.multiple_of(c * chunk, chunk)
            parts = []
            for i in range(8):
                one_up = jnp.broadcast_to(row_up[i:i + 1], (elec, width)).astype(BF16)
                one_down = jnp.broadcast_to(row_down[i:i + 1], (elec, width)).astype(BF16)
                spread = jnp.where(up_rows[...] > 0.5, one_up, one_down)
                parts.append(spread * slope[w, pl.ds(start + i * elec, elec), :])
            block = pairs[w, :, pl.ds(start, chunk)]
            for k in range(4):
                both = jnp.concatenate(parts[2 * k:2 * k + 2], axis=0)
                grad = grad + dot(block[:, k * tile:(k + 1) * tile], both)
            while len(parts) > 1:
                parts = [a + b for a, b in zip(parts[::2], parts[1::2])]
            return dkey + parts[0].astype(F32), grad

        dkey, grad_msg = lax.fori_loop(
            0, chunks, step, (jnp.zeros((elec, width), F32), grad_msg)
        )
        dkeys[here, :] = dkey.astype(BF16)
        out = incoming + dot_nt(dz, full_w[1]) + dot_nt(dkey.astype(BF16), full_w[0])
        dh[w] = out.astype(BF16)

        @pl.when(section > 0)
        def _():
            down(w).start()

        bias_msg = bias_msg + jnp.sum(dkey, axis=0, keepdims=True)
        bias_self = bias_self + jnp.sum(dz.astype(F32), axis=0, keepdims=True)
        return grad_msg, bias_msg, bias_self

    none = jnp.zeros((1, width), F32)
    grad_msg, bias_msg, bias_self = lax.fori_loop(
        0, micro, walker, (jnp.zeros((pair_width, width), F32), none, none)
    )

    lefts = (h_all, sums[0], sums[1])
    for which in range(3):
        grad = dot_tn(lefts[which], dzs[...])
        for k in range(n_walk):
            out_rest[k, which] = grad[k * rows:(k + 1) * rows].astype(BF16)
    for step in range(n_walk - 1):
        grad_copy(0, out_rest, in_rest, step, peers[step], walk).start()
    grad = dot_tn(h_all, dkeys[...])
    tail = jnp.concatenate(
        [grad_msg, bias_msg, bias_self, jnp.zeros((14, width), F32)], axis=0
    )
    for k in range(n_walk):
        out_key[k] = grad[k * rows:(k + 1) * rows].astype(BF16)
        part = tail[:, k * cols:(k + 1) * cols]
        out_msg[k] = jnp.concatenate(
            [part, jnp.zeros((tail.shape[0], 128 - cols), F32)], axis=1
        ).astype(BF16)
    for step in range(n_walk - 1):
        grad_copy(1, out_key, in_key, step, peers[step], walk).start()
        grad_copy(2, out_msg, in_msg, step, peers[step], walk).start()

    def collect(kind, out, into):
        total = out[walk].astype(F32)
        for step in range(n_walk - 1):
            grad_copy(kind, out, into, step, peers[step], peers[step]).wait_recv()
            total = total + into[peers[step]].astype(F32)
        return total * (1.0 / elec)

    rest = collect(0, out_rest, in_rest)
    gs[...] = rest[0]
    gu[...] = rest[1]
    gd[...] = rest[2]
    gk[...] = collect(1, out_key, in_key)
    last = collect(2, out_msg, in_msg)
    gm[...] = last[:pair_width, :cols]
    gbm[...] = last[pair_width:pair_width + 1, :cols]
    gbs[...] = last[pair_width + 1:pair_width + 2, :cols]

    for kind, ref in kinds:
        for step in range(n_walk - 1):
            weight_copy(kind, ref, step, walk).wait_send()
    for kind, out, into in ((0, out_rest, in_rest), (1, out_key, in_key), (2, out_msg, in_msg)):
        for step in range(n_walk - 1):
            grad_copy(kind, out, into, step, peers[step], walk).wait_send()

    @pl.when(section > 0)
    def _():
        for w in range(micro):
            down(w).wait_send()


def per_device(
    n_walk, n_section,
    states, pair_feats, top_cotangent, w_key, w_msg, b_msg, w_self, w_up, w_down, b_self, spins
):
    micro, walkers, elec, width = states.shape[1:]
    pair_width = pair_feats.shape[2]
    count = micro * walkers
    rows = w_key.shape[1]
    cols = w_msg.shape[2]
    tail = pair_width + 16
    vmem = pl.BlockSpec(memory_space=pltpu.VMEM)
    shape = jax.ShapeDtypeStruct
    outs = pl.pallas_call(
        functools.partial(kernel, n_walk, n_section),
        out_shape=(
            shape((count, elec, width), BF16),
            shape((rows, width), F32),
            shape((pair_width, cols), F32),
            shape((1, cols), F32),
            shape((rows, width), F32),
            shape((rows, width), F32),
            shape((rows, width), F32),
            shape((1, cols), F32),
        ),
        in_specs=[vmem, pl.BlockSpec(memory_space=pl.ANY)] + [vmem] * 9,
        out_specs=(vmem,) * 8,
        scratch_shapes=[
            pltpu.VMEM((count, elec * elec, width), BF16),
            pltpu.VMEM((count, pair_width, elec * elec), BF16),
            pltpu.VMEM((n_walk, rows, width), BF16),
            pltpu.VMEM((n_walk, 3, rows, width), BF16),
            pltpu.VMEM((n_walk, pair_width, 128), BF16),
            pltpu.VMEM((4, width, width), BF16),
            pltpu.VMEM((4, 2 * elec, width), BF16),
            pltpu.VMEM((2 * elec, elec), BF16),
            pltpu.VMEM((4, 16, 2 * elec), BF16),
            pltpu.VMEM((elec, width), BF16),
            pltpu.VMEM((count, elec, width), F32),
            pltpu.VMEM((count, elec, width), F32),
            pltpu.VMEM((2, count * elec, width), BF16),
            pltpu.VMEM((count, elec, width), F32),
            pltpu.VMEM((count, elec, width), BF16),
            pltpu.VMEM((count * elec, width), BF16),
            pltpu.VMEM((count * elec, width), BF16),
            pltpu.VMEM((elec, width), F32),
            pltpu.VMEM((elec, width), F32),
            pltpu.VMEM((n_walk, 3, rows, width), BF16),
            pltpu.VMEM((n_walk, 3, rows, width), BF16),
            pltpu.VMEM((n_walk, rows, width), BF16),
            pltpu.VMEM((n_walk, rows, width), BF16),
            pltpu.VMEM((n_walk, tail, 128), BF16),
            pltpu.VMEM((n_walk, tail, 128), BF16),
            pltpu.SemaphoreType.DMA((count,)),
            pltpu.SemaphoreType.DMA((3, n_walk)),
            pltpu.SemaphoreType.DMA((3, n_walk)),
            pltpu.SemaphoreType.DMA((count,)),
            pltpu.SemaphoreType.DMA((count,)),
            pltpu.SemaphoreType.DMA((3, n_walk)),
            pltpu.SemaphoreType.DMA((3, n_walk)),
        ],
        compiler_params=pltpu.CompilerParams(
            collective_id=0, has_side_effects=True, vmem_limit_bytes=58 * 1024 * 1024
        ),
    )(
        states[0].reshape(count, elec, width),
        pair_feats.reshape(count, pair_width, elec * elec),
        top_cotangent.reshape(count, elec, width),
        w_key[0], w_msg[0], b_msg, w_self[0], w_up[0], w_down[0], b_self,
        spins.reshape(1, elec),
    )
    dh, gk, gm, gbm, gs, gu, gd, gbs = outs
    return (
        dh.reshape(1, micro, walkers, elec, width),
        gk[None], gm[None], gbm, gs[None], gu[None], gd[None], gbs,
    )


def solution(mesh):
    in_specs = (
        P("section", None, ("grp", "walk"), None, None),
        P(None, ("grp", "walk"), None, None),
        P(None, ("grp", "walk"), None, None),
        P("section", "walk", None),
        P("section", None, "walk"),
        P("section", None),
        P("section", "walk", None),
        P("section", "walk", None),
        P("section", "walk", None),
        P("section", None),
        P(),
    )
    out_specs = (
        P("section", None, ("grp", "walk"), None, None),
        P(("grp", "section"), "walk", None),
        P(("grp", "section"), None, "walk"),
        P(("grp", "section"), "walk"),
        P(("grp", "section"), "walk", None),
        P(("grp", "section"), "walk", None),
        P(("grp", "section"), "walk", None),
        P(("grp", "section"), "walk"),
    )
    return jax.shard_map(
        functools.partial(per_device, mesh.shape["walk"], mesh.shape["section"]),
        mesh=mesh, in_specs=in_specs, out_specs=out_specs, check_vma=False,
    )
```

time: 1400 us -> 101 us (0.07)
  waiting for transfers between devices: 581 us -> 0 us
  matrix products: 325 us -> 0 us
  other arithmetic: 181 us -> 0 us
  local copies, waits for them, and re-layouts: 144 us -> 11.2 us
  Pallas kernels: 0 us -> 88.3 us
  blocking collectives: 81.8 us -> 0 us
  loops' own time: 48.8 us -> 0 us
    ppermute x7 -> x0, waiting for transfers between devices: 510 us -> none  [from_behind(): return lax.ppermute(shard, axis, pairs)]
    dot_general x368 -> x0, matrix products: 325 us -> none  [the longest x132 146 us: inner_product(): lax.dot_general(left, right, (((0,), (0,)), ((), ())), preferred_element_...]
    reduce_sum x64 -> x0, other arithmetic: 97.7 us -> none  [the longest x32 50.7 us: row_block(): jnp.sum(dpre_rows, axis=0, dtype=jnp.float32)]
    pallas_call x0 -> x1, Pallas kernels: none -> 88.3 us  [per_device(): pl.pallas_call(functools.partial(kernel, n_walk, n_section), out_shape=(s...]
    all_gather x5 -> x0, blocking collectives: 71.9 us -> none  [the longest x1 15.9 us: per_device(): lax.all_gather(w_key, 'walk', axis=1, tiled=True)]
    reduce_scatter x4 -> x0, waiting for transfers between devices: 70.5 us -> none  [the longest x1 18.2 us: per_device(): lax.psum_scatter(grads[4].astype(jnp.bfloat16), 'walk', scatter_dimension...]
    another operation x12 -> x0, loops' own time: 48.8 us -> none  [the longest x4 48.5 us: walker_back(): lax.scan(row_block, start_carry, jnp.arange(blocks, dtype=jnp.int32))]
    dynamic_slice x32 -> x0, local copies, waits for them, and re-layouts: 42.3 us -> none  [walker_back(): lax.scan(row_block, start_carry, jnp.arange(blocks, dtype=jnp.int32))]
  transfers between devices with their start and end apart: 12 -> 0, of which waited for: 11 -> 0; matrix products, arithmetic and copies ran while one was open for 1% -> 0% of each run, Pallas kernels for 0% -> 0%
where the time goes in v1:
time: 101 us; the launch traced here: 100 us
  Pallas kernels  88.3 us (87%)
  local copies, waits for them, and re-layouts  11.2 us (11%)
    pallas_call x1, Pallas kernels, per_device(): pl.pallas_call(functools.partial(kernel, n_walk, n_section), out_shape=(s...  88.3 us
    unnamed x8, local copies, waits for them, and re-layouts  11.2 us

profile of v1, /device:TPU:0, one launch (start us, length us, event | category | flops | bytes accessed | tf_op | source)
XLA Modules:
  0.0 100.1 jit_solution(2596718661774046653)
XLA Ops:
  0.6 88.3 %shard_map.170 = (bf16[4,128,256]{2,1,0:T(8,128)(2,1)}, f32[64,256]{1,0:T(8,128)}, f32[32,64]{1,0:T(8,128)}, f32[1,64]{1,0:T(1,128)}, f32[64,256]{1,0:T(8,128)},...) custom-call(bf16[4,128,256]{2,1,0:T(8,128)(2,1)} %bitcast.18, bf16[4,32,16384]{2,1,0:T(8,128)(2,1)} %bitcast.17, ...), custom_call_target="tpu_custom_call" | custom-call | tf_op jit(solution)/shard_map/pallas_call | solution.py:281
  88.9 1.7 %copy.28 = bf16[1,4,1,128,256]{4,3,2,1,0:T(8,128)(2,1)} copy(bf16[1,4,1,128,256]{4,3,2,1,0:T(8,128)(2,1)} %bitcast.20) | data formatting | bytes 524288
  90.6 1.5 %copy.29 = f32[1,64,256]{2,1,0:T(8,128)} copy(f32[1,64,256]{2,1,0:T(8,128)} %bitcast.24) | data formatting | bytes 131072
  92.1 1.3 %copy.30 = f32[1,32,64]{2,1,0:T(8,128)} copy(f32[1,32,64]{2,1,0:T(8,128)} %bitcast.29) | data formatting | bytes 16384
  93.4 1.2 %copy.31 = f32[1,64]{1,0:T(1,128)} copy(f32[1,64]{1,0:T(1,128)} %get-tuple-element.43) | data formatting | bytes 512
  94.6 1.5 %copy.32 = f32[1,64,256]{2,1,0:T(8,128)} copy(f32[1,64,256]{2,1,0:T(8,128)} %bitcast.23) | data formatting | bytes 131072
  96.0 1.5 %copy.33 = f32[1,64,256]{2,1,0:T(8,128)} copy(f32[1,64,256]{2,1,0:T(8,128)} %bitcast.22) | data formatting | bytes 131072
  97.5 1.5 %copy.34 = f32[1,64,256]{2,1,0:T(8,128)} copy(f32[1,64,256]{2,1,0:T(8,128)} %bitcast.21) | data formatting | bytes 131072
  99.0 1.1 %copy.35 = f32[1,64]{1,0:T(1,128)} copy(f32[1,64]{1,0:T(1,128)} %get-tuple-element.47) | data formatting | bytes 512

commit v2 on v1

--- a/solution.py
+++ b/solution.py
@@ -30,12 +30,19 @@
     return jnp.concatenate(pieces, axis=0)
 
 
+def fold(entries):
+    while entries.shape[0] > 16:
+        half = entries.shape[0] // 2
+        entries = entries[:half] + entries[half:]
+    return entries
+
+
 def kernel(
     n_walk, n_section,
     states, pairs_hbm, top, wk, wm, bm, ws, wu, wd, bs, spins,
-    dh, gk, gm, gbm, gs, gu, gd, gbs,
-    slope, pairs, got_key, got_rest, got_msg, full_w, rhs, onehot, spin_rows, up_rows,
-    sum_up_f, sum_down_f, sums, tz, arrived, dzs, dkeys, ds_up, ds_down,
+    dh, total_rest, total_key, total_msg,
+    slope, pairs, got_key, got_rest, got_msg, full_w, rhs, onehot, fold_rows, up_rows,
+    partial, sums, tz, arrived, dzs, dkeys, ds_up, ds_down,
     out_rest, in_rest, out_key, in_key, out_msg, in_msg,
     pair_sem, w_send, w_recv, p_send, p_recv, g_send, g_recv,
 ):
@@ -86,12 +93,9 @@
     j = lax.broadcasted_iota(jnp.int32, (tile, elec), 1)
     onehot[...] = jnp.where(lax.rem(q, elec) == j, 1.0, 0.0).astype(BF16)
     up = jnp.where(spins[...] == 0, 1.0, 0.0)
-    up_both = jnp.concatenate([up, up], axis=1)
-    r = lax.broadcasted_iota(jnp.int32, (16, tile), 0)
-    q = lax.broadcasted_iota(jnp.int32, (16, tile), 1)
-    chosen = jnp.where(r < 8, up_both, 1.0 - up_both)
-    for k in range(4):
-        spin_rows[k] = jnp.where(q // elec == lax.rem(r, 8) - 2 * k, chosen, 0.0).astype(BF16)
+    r = lax.broadcasted_iota(jnp.int32, fold_rows.shape, 0)
+    q = lax.broadcasted_iota(jnp.int32, fold_rows.shape, 1)
+    fold_rows[...] = jnp.where(q // 16 == r, 1.0, 0.0).astype(BF16)
     up_column = jnp.transpose(jnp.broadcast_to(up, (elec, elec)))
     up_rows[...] = jnp.concatenate([up_column] * (width // elec), axis=1).astype(BF16)
 
@@ -120,17 +124,22 @@
             block = pairs[w, :, pl.ds(start, chunk)]
             stacked = jnp.concatenate([block[:, k * tile:(k + 1) * tile] for k in range(4)], axis=0)
             left = jnp.concatenate([jnp.transpose(stacked), onehot[...]], axis=1)
-            total = jnp.zeros((16, width), F32)
             for k in range(4):
                 message = jnp.tanh(dot(left, rhs[k]).astype(BF16))
                 slope[w, pl.ds(start + k * tile, tile), :] = 1.0 - message * message
-                total = total + dot(spin_rows[k], message)
-            at = pl.ds(pl.multiple_of(c * 8, 8), 8)
-            sum_up_f[w, at, :] = total[:8] * scale
-            sum_down_f[w, at, :] = total[8:] * scale
+                for i in range(2):
+                    one = message[i * elec:(i + 1) * elec]
+                    at = pl.ds(pl.multiple_of(c * 128, 128) + (2 * k + i) * 16, 16)
+                    partial[0, at, :] = fold(one)
+                    partial[1, at, :] = fold(one * up_rows[...])
             return 0
 
-        lax.fori_loop(0, chunks, step, 0)
+        lax.fori_loop(0, chunks, step, 0, unroll=4)
+        at = pl.ds(pl.multiple_of(w * elec, elec), elec)
+        sum_both = dot(fold_rows[...], partial[0])
+        sum_up = dot(fold_rows[...], partial[1])
+        sums[0, at, :] = (sum_up * scale).astype(BF16)
+        sums[1, at, :] = ((sum_both - sum_up) * scale).astype(BF16)
         return 0
 
     lax.fori_loop(0, micro, messages, 0)
@@ -140,8 +149,6 @@
     for which in range(3):
         full_w[1 + which] = join_rows([got_rest[k, which] for k in range(n_walk)])
     flat = (micro * elec, width)
-    sums[0] = sum_up_f[...].reshape(flat).astype(BF16)
-    sums[1] = sum_down_f[...].reshape(flat).astype(BF16)
     h_all = states[...].reshape(flat)
     z = dot(h_all, full_w[1]) + dot(sums[0], full_w[2]) + dot(sums[1], full_w[3]) + bs[...]
     tanh_z = jnp.tanh(z)
@@ -196,7 +203,7 @@
             return dkey + parts[0].astype(F32), grad
 
         dkey, grad_msg = lax.fori_loop(
-            0, chunks, step, (jnp.zeros((elec, width), F32), grad_msg)
+            0, chunks, step, (jnp.zeros((elec, width), F32), grad_msg), unroll=4
         )
         dkeys[here, :] = dkey.astype(BF16)
         out = incoming + dot_nt(dz, full_w[1]) + dot_nt(dkey.astype(BF16), full_w[0])
@@ -243,15 +250,9 @@
             total = total + into[peers[step]].astype(F32)
         return total * (1.0 / elec)
 
-    rest = collect(0, out_rest, in_rest)
-    gs[...] = rest[0]
-    gu[...] = rest[1]
-    gd[...] = rest[2]
-    gk[...] = collect(1, out_key, in_key)
-    last = collect(2, out_msg, in_msg)
-    gm[...] = last[:pair_width, :cols]
-    gbm[...] = last[pair_width:pair_width + 1, :cols]
-    gbs[...] = last[pair_width + 1:pair_width + 2, :cols]
+    total_rest[...] = collect(0, out_rest, in_rest)
+    total_key[...] = collect(1, out_key, in_key)
+    total_msg[...] = collect(2, out_msg, in_msg)
 
     for kind, ref in kinds:
         for step in range(n_walk - 1):
@@ -264,6 +265,20 @@
     def _():
         for w in range(micro):
             down(w).wait_send()
+
+
+def spread_out(
+    dh_in, total_rest, total_key, total_msg, dh, gk, gm, gbm, gs, gu, gd, gbs
+):
+    pair_width, cols = gm.shape
+    dh[...] = dh_in[...]
+    gk[...] = total_key[...]
+    gs[...] = total_rest[0]
+    gu[...] = total_rest[1]
+    gd[...] = total_rest[2]
+    gm[...] = total_msg[:pair_width, :cols]
+    gbm[...] = total_msg[pair_width:pair_width + 1, :cols]
+    gbs[...] = total_msg[pair_width + 1:pair_width + 2, :cols]
 
 
 def per_device(
@@ -278,20 +293,16 @@
     tail = pair_width + 16
     vmem = pl.BlockSpec(memory_space=pltpu.VMEM)
     shape = jax.ShapeDtypeStruct
-    outs = pl.pallas_call(
+    raw = pl.pallas_call(
         functools.partial(kernel, n_walk, n_section),
         out_shape=(
             shape((count, elec, width), BF16),
-            shape((rows, width), F32),
-            shape((pair_width, cols), F32),
-            shape((1, cols), F32),
-            shape((rows, width), F32),
-            shape((rows, width), F32),
-            shape((rows, width), F32),
-            shape((1, cols), F32),
+            shape((3, rows, width), F32),
+            shape((rows, width), F32),
+            shape((tail, 128), F32),
         ),
         in_specs=[vmem, pl.BlockSpec(memory_space=pl.ANY)] + [vmem] * 9,
-        out_specs=(vmem,) * 8,
+        out_specs=(vmem,) * 4,
         scratch_shapes=[
             pltpu.VMEM((count, elec * elec, width), BF16),
             pltpu.VMEM((count, pair_width, elec * elec), BF16),
@@ -301,10 +312,9 @@
             pltpu.VMEM((4, width, width), BF16),
             pltpu.VMEM((4, 2 * elec, width), BF16),
             pltpu.VMEM((2 * elec, elec), BF16),
-            pltpu.VMEM((4, 16, 2 * elec), BF16),
+            pltpu.VMEM((elec, 16 * elec), BF16),
             pltpu.VMEM((elec, width), BF16),
-            pltpu.VMEM((count, elec, width), F32),
-            pltpu.VMEM((count, elec, width), F32),
+            pltpu.VMEM((2, 16 * elec, width), BF16),
             pltpu.VMEM((2, count * elec, width), BF16),
             pltpu.VMEM((count, elec, width), F32),
             pltpu.VMEM((count, elec, width), BF16),
@@ -336,7 +346,21 @@
         w_key[0], w_msg[0], b_msg, w_self[0], w_up[0], w_down[0], b_self,
         spins.reshape(1, elec),
     )
-    dh, gk, gm, gbm, gs, gu, gd, gbs = outs
+    dh, gk, gm, gbm, gs, gu, gd, gbs = pl.pallas_call(
+        spread_out,
+        out_shape=(
+            shape((count, elec, width), BF16),
+            shape((rows, width), F32),
+            shape((pair_width, cols), F32),
+            shape((1, cols), F32),
+            shape((rows, width), F32),
+            shape((rows, width), F32),
+            shape((rows, width), F32),
+            shape((1, cols), F32),
+        ),
+        in_specs=[vmem] * 4,
+        out_specs=(vmem,) * 8,
+    )(*raw)
     return (
         dh.reshape(1, micro, walkers, elec, width),
         gk[None], gm[None], gbm, gs[None], gu[None], gd[None], gbs,

time: 101 us -> 68.9 us (0.68)
  Pallas kernels: 88.3 us -> 68.1 us
  local copies, waits for them, and re-layouts: 11.2 us -> 0 us
    pallas_call x1, Pallas kernels: 88.3 us -> 66.2 us  [per_device(): pl.pallas_call(functools.partial(kernel, n_walk, n_section), out_shape=(s...]
    unnamed x8 -> x0, local copies, waits for them, and re-layouts: 11.2 us -> none
    pallas_call x0 -> x1, Pallas kernels: none -> 1.85 us  [per_device(): pl.pallas_call(spread_out, out_shape=(shape((count, elec, width), BF16),...]
where the time goes in v2:
time: 68.9 us; the launch traced here: 68.7 us
  Pallas kernels  68.1 us (99%)
    pallas_call x1, Pallas kernels, per_device(): pl.pallas_call(functools.partial(kernel, n_walk, n_section), out_shape=(s...  66.2 us
    pallas_call x1, Pallas kernels, per_device(): pl.pallas_call(spread_out, out_shape=(shape((count, elec, width), BF16),...  1.85 us

profile of v2, /device:TPU:0, one launch (start us, length us, event | category | flops | bytes accessed | tf_op | source)
XLA Modules:
  0.0 68.7 jit_solution(7152032882572566579)
XLA Ops:
  0.6 66.2 %shard_map.170 = (bf16[4,128,256]{2,1,0:T(8,128)(2,1)}, f32[3,64,256]{2,1,0:T(8,128)}, f32[64,256]{1,0:T(8,128)}, f32[48,128]{1,0:T(8,128)}) custom-call(bf16[4,128,256]{2,1,0:T(8,128)(2,1)} %bitcast.18, bf16[4,32,16384]{2,1,0:T(8,128)(2,1)} %bitcast.17, bf16[4,128,256]{2,1,0:T(8,128)(2,1)} %bitcast.19, bf16[64,256]{1,0:T(8,128)(2,1)} %bitcast.20, ...), custom_call_target="tpu_custom_call" | custom-call | tf_op jit(solution)/shard_map/pallas_call | solution.py:296
  66.9 1.9 %shard_map.171 = (bf16[4,128,256]{2,1,0:T(8,128)(2,1)}, f32[64,256]{1,0:T(8,128)}, f32[32,64]{1,0:T(8,128)}, f32[1,64]{1,0:T(1,128)}, f32[64,256]{1,0:T(8,128)},...) custom-call(bf16[4,128,256]{2,1,0:T(8,128)(2,1)} %get-tuple-element.20.dh_in, ...), custom_call_target="tpu_custom_call" | custom-call | tf_op jit(solution)/shard_map/pallas_call | solution.py:349

commit v3 on v2

--- a/solution.py
+++ b/solution.py
@@ -42,7 +42,7 @@
     states, pairs_hbm, top, wk, wm, bm, ws, wu, wd, bs, spins,
     dh, total_rest, total_key, total_msg,
     slope, pairs, got_key, got_rest, got_msg, full_w, rhs, onehot, fold_rows, up_rows,
-    partial, sums, tz, arrived, dzs, dkeys, ds_up, ds_down,
+    partial, sums, tz, arrived, dzs, dkeys, ds_up, ds_down, tail, grads,
     out_rest, in_rest, out_key, in_key, out_msg, in_msg,
     pair_sem, w_send, w_recv, p_send, p_recv, g_send, g_recv,
 ):
@@ -113,47 +113,6 @@
         after = [jnp.zeros(((3 - k) * pair_width, width), BF16)] if k < 3 else []
         rhs[k, 0:elec] = jnp.concatenate(before + [w_msg] + after, axis=0)
 
-    def messages(w, _):
-        pltpu.make_async_copy(pairs_hbm.at[w], pairs.at[w], pair_sem.at[w]).wait()
-        keyed = (dot(states[w], full_w[0]) + bm[...]).astype(BF16)
-        for k in range(4):
-            rhs[k, elec:] = keyed
-
-        def step(c, _):
-            start = pl.multiple_of(c * chunk, chunk)
-            block = pairs[w, :, pl.ds(start, chunk)]
-            stacked = jnp.concatenate([block[:, k * tile:(k + 1) * tile] for k in range(4)], axis=0)
-            left = jnp.concatenate([jnp.transpose(stacked), onehot[...]], axis=1)
-            for k in range(4):
-                message = jnp.tanh(dot(left, rhs[k]).astype(BF16))
-                slope[w, pl.ds(start + k * tile, tile), :] = 1.0 - message * message
-                for i in range(2):
-                    one = message[i * elec:(i + 1) * elec]
-                    at = pl.ds(pl.multiple_of(c * 128, 128) + (2 * k + i) * 16, 16)
-                    partial[0, at, :] = fold(one)
-                    partial[1, at, :] = fold(one * up_rows[...])
-            return 0
-
-        lax.fori_loop(0, chunks, step, 0, unroll=4)
-        at = pl.ds(pl.multiple_of(w * elec, elec), elec)
-        sum_both = dot(fold_rows[...], partial[0])
-        sum_up = dot(fold_rows[...], partial[1])
-        sums[0, at, :] = (sum_up * scale).astype(BF16)
-        sums[1, at, :] = ((sum_both - sum_up) * scale).astype(BF16)
-        return 0
-
-    lax.fori_loop(0, micro, messages, 0)
-
-    for step in range(n_walk - 1):
-        weight_copy(2, got_rest, step, peers[step]).wait_recv()
-    for which in range(3):
-        full_w[1 + which] = join_rows([got_rest[k, which] for k in range(n_walk)])
-    flat = (micro * elec, width)
-    h_all = states[...].reshape(flat)
-    z = dot(h_all, full_w[1]) + dot(sums[0], full_w[2]) + dot(sums[1], full_w[3]) + bs[...]
-    tanh_z = jnp.tanh(z)
-    tz[...] = (1.0 - tanh_z * tanh_z).reshape(micro, elec, width)
-
     def down(w):
         return pltpu.make_async_remote_copy(
             src_ref=dh.at[w], dst_ref=arrived.at[w],
@@ -168,19 +127,14 @@
             device_id={"walk": peers[step]}, device_id_type=MESH,
         )
 
-    def walker(w, carry):
-        grad_msg, bias_msg, bias_self = carry
-
-        @pl.when(section < n_section - 1)
-        def _():
-            down(w).wait_recv()
-
-        incoming = arrived[w].astype(F32)
-        dz = (incoming * tz[w]).astype(BF16)
-        here = pl.ds(pl.multiple_of(w * elec, elec), elec)
-        dzs[here, :] = dz
+    def begin(w):
+        dz = (arrived[w].astype(F32) * tz[w]).astype(BF16)
+        dzs[pl.ds(pl.multiple_of(w * elec, elec), elec), :] = dz
         ds_up[...] = dot_nt(dz, full_w[2]) * scale
         ds_down[...] = dot_nt(dz, full_w[3]) * scale
+
+    def finish(w):
+        here = pl.ds(pl.multiple_of(w * elec, elec), elec)
 
         def step(c, carry):
             dkey, grad = carry
@@ -202,40 +156,120 @@
                 parts = [a + b for a, b in zip(parts[::2], parts[1::2])]
             return dkey + parts[0].astype(F32), grad
 
-        dkey, grad_msg = lax.fori_loop(
-            0, chunks, step, (jnp.zeros((elec, width), F32), grad_msg), unroll=4
+        dkey, grad = lax.fori_loop(
+            0, chunks, step,
+            (jnp.zeros((elec, width), F32), jnp.zeros((pair_width, width), F32)), unroll=8,
         )
         dkeys[here, :] = dkey.astype(BF16)
-        out = incoming + dot_nt(dz, full_w[1]) + dot_nt(dkey.astype(BF16), full_w[0])
-        dh[w] = out.astype(BF16)
+        out = arrived[w].astype(F32) + dot_nt(dzs[here, :], full_w[1])
+        dh[w] = (out + dot_nt(dkey.astype(BF16), full_w[0])).astype(BF16)
 
         @pl.when(section > 0)
         def _():
             down(w).start()
 
-        bias_msg = bias_msg + jnp.sum(dkey, axis=0, keepdims=True)
-        bias_self = bias_self + jnp.sum(dz.astype(F32), axis=0, keepdims=True)
-        return grad_msg, bias_msg, bias_self
-
-    none = jnp.zeros((1, width), F32)
-    grad_msg, bias_msg, bias_self = lax.fori_loop(
-        0, micro, walker, (jnp.zeros((pair_width, width), F32), none, none)
-    )
-
-    lefts = (h_all, sums[0], sums[1])
+        tail[0:pair_width, :] += grad
+        tail[pair_width:pair_width + 1, :] += jnp.sum(dkey, axis=0, keepdims=True)
+        tail[pair_width + 1:pair_width + 2, :] += jnp.sum(
+            dzs[here, :].astype(F32), axis=0, keepdims=True
+        )
+
+    def messages(w, _):
+        pltpu.make_async_copy(pairs_hbm.at[w], pairs.at[w], pair_sem.at[w]).wait()
+        keyed = (dot(states[w], full_w[0]) + bm[...]).astype(BF16)
+        for k in range(4):
+            rhs[k, elec:] = keyed
+
+        def step(c, _):
+            start = pl.multiple_of(c * chunk, chunk)
+            block = pairs[w, :, pl.ds(start, chunk)]
+            stacked = jnp.concatenate([block[:, k * tile:(k + 1) * tile] for k in range(4)], axis=0)
+            left = jnp.concatenate([jnp.transpose(stacked), onehot[...]], axis=1)
+            for k in range(4):
+                message = jnp.tanh(dot(left, rhs[k]).astype(BF16))
+                slope[w, pl.ds(start + k * tile, tile), :] = 1.0 - message * message
+                for i in range(2):
+                    one = message[i * elec:(i + 1) * elec]
+                    at = pl.ds(pl.multiple_of(c * 128, 128) + (2 * k + i) * 16, 16)
+                    partial[0, at, :] = fold(one)
+                    partial[1, at, :] = fold(one * up_rows[...])
+            return 0
+
+        lax.fori_loop(0, chunks, step, 0, unroll=4)
+        at = pl.ds(pl.multiple_of(w * elec, elec), elec)
+        sum_both = dot(fold_rows[...], partial[0])
+        sum_up = dot(fold_rows[...], partial[1])
+        sums[0, at, :] = (sum_up * scale).astype(BF16)
+        sums[1, at, :] = ((sum_both - sum_up) * scale).astype(BF16)
+
+        @pl.when(w == 0)
+        def _():
+            for step in range(n_walk - 1):
+                weight_copy(2, got_rest, step, peers[step]).wait_recv()
+            for which in range(3):
+                full_w[1 + which] = join_rows([got_rest[k, which] for k in range(n_walk)])
+
+        z = dot(states[w], full_w[1]) + dot(sums[0, at, :], full_w[2])
+        tanh_z = jnp.tanh(z + dot(sums[1, at, :], full_w[3]) + bs[...])
+        tz[w] = 1.0 - tanh_z * tanh_z
+
+        @pl.when(section == n_section - 1)
+        def _():
+            begin(w)
+            finish(w)
+
+        return 0
+
+    tail[...] = jnp.zeros_like(tail)
+    lax.fori_loop(0, micro, messages, 0)
+
+    final = micro - 1
+    below_top = section < n_section - 1
+
+    @pl.when(below_top)
+    def _():
+        def walker(w, _):
+            down(w).wait_recv()
+            begin(w)
+            finish(w)
+            return 0
+
+        lax.fori_loop(0, final, walker, 0)
+
+    first = slice(0, final * elec)
+    last = slice(final * elec, micro * elec)
+    h_first = states[0:final].reshape(final * elec, width)
+    h_last = states[final]
+    grads[0] = dot_tn(h_first, dzs[first, :])
+    grads[1] = dot_tn(sums[0, first, :], dzs[first, :])
+    grads[2] = dot_tn(sums[1, first, :], dzs[first, :])
+    grads[3] = dot_tn(h_first, dkeys[first, :])
+
+    @pl.when(below_top)
+    def _():
+        down(final).wait_recv()
+        begin(final)
+
+    @pl.when(jnp.logical_and(below_top, section > 0))
+    def _():
+        finish(final)
+
+    lefts = (h_last, sums[0, last, :], sums[1, last, :])
     for which in range(3):
-        grad = dot_tn(lefts[which], dzs[...])
+        grad = grads[which] + dot_tn(lefts[which], dzs[last, :])
         for k in range(n_walk):
             out_rest[k, which] = grad[k * rows:(k + 1) * rows].astype(BF16)
     for step in range(n_walk - 1):
         grad_copy(0, out_rest, in_rest, step, peers[step], walk).start()
-    grad = dot_tn(h_all, dkeys[...])
-    tail = jnp.concatenate(
-        [grad_msg, bias_msg, bias_self, jnp.zeros((14, width), F32)], axis=0
-    )
+
+    @pl.when(section == 0)
+    def _():
+        finish(final)
+
+    grad = grads[3] + dot_tn(h_last, dkeys[last, :])
     for k in range(n_walk):
         out_key[k] = grad[k * rows:(k + 1) * rows].astype(BF16)
-        part = tail[:, k * cols:(k + 1) * cols]
+        part = tail[...][:, k * cols:(k + 1) * cols]
         out_msg[k] = jnp.concatenate(
             [part, jnp.zeros((tail.shape[0], 128 - cols), F32)], axis=1
         ).astype(BF16)
@@ -322,6 +356,8 @@
             pltpu.VMEM((count * elec, width), BF16),
             pltpu.VMEM((elec, width), F32),
             pltpu.VMEM((elec, width), F32),
+            pltpu.VMEM((tail, width), F32),
+            pltpu.VMEM((4, width, width), F32),
             pltpu.VMEM((n_walk, 3, rows, width), BF16),
             pltpu.VMEM((n_walk, 3, rows, width), BF16),
             pltpu.VMEM((n_walk, rows, width), BF16),

time: 68.9 us -> 68.6 us (level)
  no operation moved by 1% of the time
where the time goes in v3:
time: 68.6 us; the launch traced here: 68.3 us
  Pallas kernels  67.6 us (99%)
    pallas_call x1, Pallas kernels, per_device(): pl.pallas_call(functools.partial(kernel, n_walk, n_section), out_shape=(s...  65.8 us
    pallas_call x1, Pallas kernels, per_device(): pl.pallas_call(spread_out, out_shape=(shape((count, elec, width), BF16),...  1.85 us

profile of v3, /device:TPU:0, one launch (start us, length us, event | category | flops | bytes accessed | tf_op | source)
XLA Modules:
  0.0 68.3 jit_solution(7371555314506283657)
XLA Ops:
  0.6 65.8 %shard_map.170 = (bf16[4,128,256]{2,1,0:T(8,128)(2,1)}, f32[3,64,256]{2,1,0:T(8,128)}, f32[64,256]{1,0:T(8,128)}, f32[48,128]{1,0:T(8,128)}) custom-call(bf16[4,128,256]{2,1,0:T(8,128)(2,1)} %bitcast.18, bf16[4,32,16384]{2,1,0:T(8,128)(2,1)} %bitcast.17, bf16[4,128,256]{2,1,0:T(8,128)(2,1)} %bitcast.19, bf16[64,256]{1,0:T(8,128)(2,1)} %bitcast.20, ...), custom_call_target="tpu_custom_call" | custom-call | tf_op jit(solution)/shard_map/pallas_call | solution.py:330
  66.4 1.9 %shard_map.171 = (bf16[4,128,256]{2,1,0:T(8,128)(2,1)}, f32[64,256]{1,0:T(8,128)}, f32[32,64]{1,0:T(8,128)}, f32[1,64]{1,0:T(1,128)}, f32[64,256]{1,0:T(8,128)},...) custom-call(bf16[4,128,256]{2,1,0:T(8,128)(2,1)} %get-tuple-element.20.dh_in, ...), custom_call_target="tpu_custom_call" | custom-call | tf_op jit(solution)/shard_map/pallas_call | solution.py:385

commit v4 on v3

--- a/solution.py
+++ b/solution.py
@@ -127,14 +127,17 @@
             device_id={"walk": peers[step]}, device_id_type=MESH,
         )
 
+    def rows_of(w):
+        return pl.ds(w * elec if isinstance(w, int) else pl.multiple_of(w * elec, elec), elec)
+
     def begin(w):
         dz = (arrived[w].astype(F32) * tz[w]).astype(BF16)
-        dzs[pl.ds(pl.multiple_of(w * elec, elec), elec), :] = dz
+        dzs[rows_of(w), :] = dz
         ds_up[...] = dot_nt(dz, full_w[2]) * scale
         ds_down[...] = dot_nt(dz, full_w[3]) * scale
 
     def finish(w):
-        here = pl.ds(pl.multiple_of(w * elec, elec), elec)
+        here = rows_of(w)
 
         def step(c, carry):
             dkey, grad = carry
@@ -196,19 +199,27 @@
             return 0
 
         lax.fori_loop(0, chunks, step, 0, unroll=4)
-        at = pl.ds(pl.multiple_of(w * elec, elec), elec)
+        at = rows_of(w)
         sum_both = dot(fold_rows[...], partial[0])
         sum_up = dot(fold_rows[...], partial[1])
         sums[0, at, :] = (sum_up * scale).astype(BF16)
         sums[1, at, :] = ((sum_both - sum_up) * scale).astype(BF16)
 
-        @pl.when(w == 0)
+        @pl.when(w == 1)
         def _():
             for step in range(n_walk - 1):
                 weight_copy(2, got_rest, step, peers[step]).wait_recv()
             for which in range(3):
                 full_w[1 + which] = join_rows([got_rest[k, which] for k in range(n_walk)])
 
+        @pl.when(w > 0)
+        def _():
+            settle(w - 1)
+
+        return 0
+
+    def settle(w):
+        at = rows_of(w)
         z = dot(states[w], full_w[1]) + dot(sums[0, at, :], full_w[2])
         tanh_z = jnp.tanh(z + dot(sums[1, at, :], full_w[3]) + bs[...])
         tz[w] = 1.0 - tanh_z * tanh_z
@@ -218,10 +229,9 @@
             begin(w)
             finish(w)
 
-        return 0
-
     tail[...] = jnp.zeros_like(tail)
     lax.fori_loop(0, micro, messages, 0)
+    settle(micro - 1)
 
     final = micro - 1
     below_top = section < n_section - 1

time: 68.6 us -> 68.2 us (level)
  no operation moved by 1% of the time
where the time goes in v4:
time: 68.2 us; the launch traced here: 67.6 us
  Pallas kernels  67 us (98%)
    pallas_call x1, Pallas kernels, per_device(): pl.pallas_call(functools.partial(kernel, n_walk, n_section), out_shape=(s...  65.1 us
    pallas_call x1, Pallas kernels, per_device(): pl.pallas_call(spread_out, out_shape=(shape((count, elec, width), BF16),...  1.85 us

profile of v4, /device:TPU:0, one launch (start us, length us, event | category | flops | bytes accessed | tf_op | source)
XLA Modules:
  0.0 67.6 jit_solution(11037552472305395383)
XLA Ops:
  0.6 65.1 %shard_map.170 = (bf16[4,128,256]{2,1,0:T(8,128)(2,1)}, f32[3,64,256]{2,1,0:T(8,128)}, f32[64,256]{1,0:T(8,128)}, f32[48,128]{1,0:T(8,128)}) custom-call(bf16[4,128,256]{2,1,0:T(8,128)(2,1)} %bitcast.18, bf16[4,32,16384]{2,1,0:T(8,128)(2,1)} %bitcast.17, bf16[4,128,256]{2,1,0:T(8,128)(2,1)} %bitcast.19, bf16[64,256]{1,0:T(8,128)(2,1)} %bitcast.20, ...), custom_call_target="tpu_custom_call" | custom-call | tf_op jit(solution)/shard_map/pallas_call | solution.py:340
  65.8 1.9 %shard_map.171 = (bf16[4,128,256]{2,1,0:T(8,128)(2,1)}, f32[64,256]{1,0:T(8,128)}, f32[32,64]{1,0:T(8,128)}, f32[1,64]{1,0:T(1,128)}, f32[64,256]{1,0:T(8,128)},...) custom-call(bf16[4,128,256]{2,1,0:T(8,128)(2,1)} %get-tuple-element.20.dh_in, ...), custom_call_target="tpu_custom_call" | custom-call | tf_op jit(solution)/shard_map/pallas_call | solution.py:395
